TPU v7x, 32 devices: a whole 2x2x4 slice. The times are simulated.
32 devices in a mesh: seq: 8 (over z, x), head: 4 (over y, core).
Axes of the slice: x: 2, y: 2, z: 4, core: 2. Of those that a mesh axis runs over, the one named last changes fastest.
Arguments:
- query_rows: bfloat16 [16384, 1024], P('seq', 'head'), may hold values from -6 to 6
- key_rows: bfloat16 [16384, 1024], P('seq', 'head'), may hold values from -6 to 6
- value_rows: bfloat16 [16384, 1024], P('seq', 'head'), may hold values from -24 to 24
- norm_gain: bfloat16 [1024], P('head'), may hold values from 0.5 to 1.5
Outputs:
- attended: bfloat16 [16384, 1024], P('seq', 'head')
All inputs are finite; a program needn't handle non-finite values.
Results may differ from a plain program's by a relative error of at most 0.01.
Values may be sent and summed in bfloat16 or wider, within the bound.
A program may use at most 192 MiB of HBM per device.

v0:
```python
import functools
import math

import jax
import jax.numpy as jnp
from jax import lax
from jax.experimental import pallas as pl
from jax.experimental.pallas import tpu as pltpu
from jax.sharding import PartitionSpec as P

D = 1024
HEAD_DIM = 64
BLOCK = 1024
LEVELS = 3
TOP_POOL = 32
QUERY_TILE = 256
CHUNK = 256
LANES = 128
LOG2E = math.log2(math.e)
MESH = pl.DeviceIdType.MESH


def pool_matrix(factors):
    pieces = []
    for factor in factors:
        shape = (CHUNK // factor, CHUNK)
        row = lax.broadcasted_iota(jnp.int32, shape, 0)
        window = lax.broadcasted_iota(jnp.int32, shape, 1) // factor
        pieces.append(jnp.where(window == row, 1.0 / factor, 0.0))
    return jnp.concatenate(pieces, axis=0).astype(jnp.bfloat16)


def kernel(n_seq, n_head, q_ref, k_ref, v_ref, g_ref, o_ref,
           near, far, acc, high, ctx, squares,
           level_send, level_recv, coarse_send, coarse_recv, square_send, square_recv):
    tokens, width = q_ref.shape
    heads = width // HEAD_DIM
    coarse_rows = tokens // TOP_POOL
    coarse_all = coarse_rows * n_seq
    me_seq = lax.axis_index("seq")
    me_head = lax.axis_index("head")

    def seq_peer(step):
        return lax.rem(me_seq + step, n_seq)

    def head_peer(step):
        return lax.rem(me_head + step, n_head)

    barrier = pltpu.get_barrier_semaphore()

    @pl.loop(1, n_seq)
    def _(step):
        pl.semaphore_signal(barrier, inc=1, device_id=(seq_peer(step), me_head), device_id_type=MESH)

    @pl.loop(1, n_head)
    def _(step):
        pl.semaphore_signal(barrier, inc=1, device_id=(me_seq, head_peer(step)), device_id_type=MESH)

    factors = [2**level for level in range(1, LEVELS + 1)]
    level_rows = {f: tokens // f for f in factors}
    near_at, far_at, first_row = {}, {}, 0
    for f in reversed(factors):
        near_at[f] = first_row
        far_at[f] = coarse_all + first_row
        first_row += level_rows[f]
    matrix = pool_matrix(factors + [TOP_POOL])
    for side, source in enumerate((k_ref, v_ref)):
        columns = pl.ds(side * width, width)
        held = []
        for chunk in range(tokens // CHUNK):
            pooled = jnp.dot(matrix, source[pl.ds(chunk * CHUNK, CHUNK), :],
                             preferred_element_type=jnp.float32)
            start = 0
            for f in factors:
                size = CHUNK // f
                near[pl.ds(near_at[f] + chunk * size, size), columns] = (
                    pooled[start:start + size].astype(jnp.bfloat16))
                start += size
            held.append(pooled[start:])
        far[pl.ds(pl.multiple_of(me_seq * coarse_rows, coarse_rows), coarse_rows), columns] = (
            jnp.concatenate(held, axis=0).astype(jnp.bfloat16))

    pl.semaphore_wait(barrier, n_seq - 1 + n_head - 1)

    def level_copy(level):
        f = 2**level
        distance = 2 ** (level - 1)
        partner = me_seq + distance * (1 - 2 * lax.rem(me_seq // distance, 2))
        return pltpu.make_async_remote_copy(
            src_ref=near.at[pl.ds(near_at[f], level_rows[f])],
            dst_ref=far.at[pl.ds(far_at[f], level_rows[f])],
            send_sem=level_send.at[level - 1],
            recv_sem=level_recv.at[level - 1],
            device_id=(partner, me_head),
            device_id_type=MESH,
        )

    def coarse_copy(step):
        mine = far.at[pl.ds(pl.multiple_of(me_seq * coarse_rows, coarse_rows), coarse_rows)]
        return pltpu.make_async_remote_copy(
            src_ref=mine,
            dst_ref=mine,
            send_sem=coarse_send.at[step],
            recv_sem=coarse_recv.at[step],
            device_id=(seq_peer(step), me_head),
            device_id_type=MESH,
        )

    @pl.loop(1, n_seq)
    def _(step):
        coarse_copy(step).start()

    level_copies = {level: level_copy(level) for level in range(1, LEVELS + 1)}
    for level in (1, 3, 2):
        level_copies[level].start()

    lane_head = lax.broadcasted_iota(jnp.int32, (1, width), 1) // HEAD_DIM
    scaled_masks = [
        jnp.where(lane_head == h, 1.0 / math.sqrt(HEAD_DIM), 0.0).astype(jnp.bfloat16)
        for h in range(heads)
    ]
    left = lax.broadcasted_iota(jnp.int32, (QUERY_TILE, LANES), 1) < HEAD_DIM

    def attend(tile, keys, values, first, last):
        rows = pl.ds(pl.multiple_of(tile * QUERY_TILE, QUERY_TILE), QUERY_TILE)
        query = q_ref[rows, :]
        ones = jnp.ones((keys.shape[0], LANES), jnp.bfloat16)

        def scores(h):
            return lax.dot_general(query * scaled_masks[h], keys, (((1,), (1,)), ((), ())),
                                   preferred_element_type=jnp.float32)

        ready = scores(0)
        shares = []
        for h in range(heads):
            score = ready
            if h + 1 < heads:
                ready = scores(h + 1)
            highest = jnp.max(score, axis=-1, keepdims=True)
            if not first:
                before = high[h, rows, :]
                highest = jnp.maximum(before[:, :1], highest)
            weights = jnp.exp2((score - highest) * LOG2E).astype(jnp.bfloat16)
            pair = (h // 2) * LANES
            summed = jnp.dot(weights, jnp.concatenate([values[:, pair:pair + LANES], ones], axis=1),
                             preferred_element_type=jnp.float32)
            if not first:
                factor = jnp.exp2((before[:, :1] - highest) * LOG2E)
                summed = summed + acc[h, rows, :] * factor
            if last:
                shares.append(summed[:, :LANES] / summed[:, LANES:])
            else:
                acc[h, rows, :] = summed
                high[h, rows, :] = jnp.broadcast_to(highest, (QUERY_TILE, LANES))
        if last:
            total = jnp.zeros((QUERY_TILE, LANES), jnp.float32)
            for pair in range(heads // 2):
                part = jnp.where(left, shares[2 * pair], shares[2 * pair + 1])
                ctx[rows, pl.ds(pair * LANES, LANES)] = part
                total += part * part
            total = jnp.broadcast_to(jnp.sum(total, axis=-1, keepdims=True), (QUERY_TILE, LANES))
            for piece in range(QUERY_TILE // LANES):
                turned = jnp.transpose(total[piece * LANES:(piece + 1) * LANES])
                squares[0, pl.ds(tile * (QUERY_TILE // LANES) + piece, 1), :] = turned[:1]

    tiles = tokens // QUERY_TILE

    @pl.loop(0, tiles)
    def _(tile):
        block = pl.ds(pl.multiple_of(tile * QUERY_TILE // BLOCK * BLOCK, BLOCK), BLOCK)
        attend(tile, k_ref[block, :], v_ref[block, :], True, False)

    def attend_far(start, size, last):
        @pl.loop(0, tiles)
        def _(tile):
            attend(tile, far[start:start + size, :width], far[start:start + size, width:], False, last)

    @pl.loop(1, n_seq)
    def _(step):
        coarse_copy(step).wait()

    level_copies[3].wait()
    attend_far(0, coarse_all + level_rows[8], False)
    level_copies[2].wait()
    attend_far(far_at[4], level_rows[4], False)
    level_copies[1].wait()
    attend_far(far_at[2], level_rows[2], True)

    square_copies = [
        pltpu.make_async_remote_copy(
            src_ref=squares.at[0],
            dst_ref=squares.at[step],
            send_sem=square_send.at[step],
            recv_sem=square_recv.at[step],
            device_id=(me_seq, head_peer(step)),
            device_id_type=MESH,
        )
        for step in range(1, n_head)
    ]
    for copy in square_copies:
        copy.start()
    for copy in square_copies:
        copy.wait()
    square_total = squares[0]
    for step in range(1, n_head):
        square_total = square_total + squares[step]
    inverse = lax.rsqrt(square_total / (width * n_head) + 1e-6)
    gain = g_ref[...].astype(jnp.float32)
    for piece in range(tokens // LANES):
        rows = pl.ds(piece * LANES, LANES)
        turned = jnp.transpose(jnp.broadcast_to(inverse[piece:piece + 1], (LANES, LANES)))
        for part in range(width // LANES):
            columns = pl.ds(part * LANES, LANES)
            o_ref[rows, columns] = (
                ctx[rows, columns] * turned * gain[:, part * LANES:(part + 1) * LANES]
            ).astype(jnp.bfloat16)


def body(n_seq, n_head, query_rows, key_rows, value_rows, norm_gain):
    tokens, width = query_rows.shape
    heads = width // HEAD_DIM
    level_total = sum(tokens // 2**level for level in range(1, LEVELS + 1))
    coarse_all = tokens // TOP_POOL * n_seq
    keys = BLOCK + level_total + coarse_all
    vmem = pl.BlockSpec(memory_space=pltpu.VMEM)
    dma = pltpu.SemaphoreType.DMA
    return pl.pallas_call(
        functools.partial(kernel, n_seq, n_head),
        out_shape=jax.ShapeDtypeStruct((tokens, width), jnp.bfloat16),
        in_specs=[vmem] * 4,
        out_specs=vmem,
        scratch_shapes=[
            pltpu.VMEM((level_total, 2 * width), jnp.bfloat16),
            pltpu.VMEM((coarse_all + level_total, 2 * width), jnp.bfloat16),
            pltpu.VMEM((heads, tokens, 2 * LANES), jnp.float32),
            pltpu.VMEM((heads, tokens, LANES), jnp.float32),
            pltpu.VMEM((tokens, width), jnp.float32),
            pltpu.VMEM((n_head, tokens // LANES, LANES), jnp.float32),
            dma((LEVELS,)),
            dma((LEVELS,)),
            dma((n_seq,)),
            dma((n_seq,)),
            dma((n_head,)),
            dma((n_head,)),
        ],
        compiler_params=pltpu.CompilerParams(
            collective_id=0, has_side_effects=True, vmem_limit_bytes=56 * 1024 * 1024
        ),
        cost_estimate=pl.CostEstimate(
            flops=4 * tokens * keys * width,
            bytes_accessed=8 * tokens * width,
            transcendentals=tokens * keys * heads,
        ),
    )(query_rows, key_rows, value_rows, norm_gain.reshape(1, width))


def solution(mesh):
    placed = (P("seq", "head"), P("seq", "head"), P("seq", "head"), P("head"))
    return jax.shard_map(
        functools.partial(body, mesh.shape["seq"], mesh.shape["head"]),
        mesh=mesh, in_specs=placed, out_specs=P("seq", "head"), check_vma=False,
    )
```

profile of v0, /device:TPU:0, one launch (start us, length us, event | category | flops | bytes accessed | tf_op | source)
XLA Modules:
  0.0 77.3 jit_solution(5861710130343710747)
XLA Ops:
  0.0 1.2 %reshape.3.g_ref = bf16[1,256]{1,0:T(2,128)(2,1)} reshape(bf16[256]{0:T(256)(128)(2,1)} %param.7) | data formatting | bytes 1024 | tf_op jit(solution)/shard_map/reshape | solution.py:254
  1.2 73.8 %shard_map.46 = bf16[2048,256]{1,0:T(8,128)(2,1)} custom-call(bf16[2048,256]{1,0:T(8,128)(2,1)} %q_ref.1, bf16[2048,256]{1,0:T(8,128)(2,1)} %k_ref.1, bf16[2048,256]{1,0:T(8,128)(2,1)} %v_ref.1, bf16[1,256]{1,0:T(2,128)(2,1)} %reshape.3.g_ref), custom_call_target="tpu_custom_call" | custom-call | flops 6979321856 | bytes 4194304 | tf_op jit(solution)/shard_map/pallas_call | solution.py:227
  75.0 2.3 %copy.6 = bf16[2048,256]{1,0:T(8,128)(2,1)} copy(bf16[2048,256]{1,0:T(8,128)(2,1)} %shard_map.46) | data formatting | bytes 2097152
where the time goes:
time: 77.5 us; the launch traced here: 77.3 us
  Pallas kernels  73.8 us (95%)
  local copies, waits for them, and re-layouts  3.48 us (4%)
    pallas_call x1, Pallas kernels, body(): pl.pallas_call(functools.partial(kernel, n_seq, n_head), out_shape=jax.Sh...  73.8 us
    unnamed x1, local copies, waits for them, and re-layouts  2.26 us

commit v1 on v0

--- a/solution.py
+++ b/solution.py
@@ -13,7 +13,7 @@
 BLOCK = 1024
 LEVELS = 3
 TOP_POOL = 32
-QUERY_TILE = 256
+QUERY_TILE = 512
 CHUNK = 256
 LANES = 128
 LOG2E = math.log2(math.e)
@@ -30,10 +30,12 @@
     return jnp.concatenate(pieces, axis=0).astype(jnp.bfloat16)
 
 
-def kernel(n_seq, n_head, q_ref, k_ref, v_ref, g_ref, o_ref,
-           near, far, acc, high, ctx, squares,
-           level_send, level_recv, coarse_send, coarse_recv, square_send, square_recv):
+def kernel(n_seq, n_head, q_hbm, k_ref, v_ref, ctx_hbm, inverse_ref,
+           q_ref, near, far, acc, high, ctx, squares,
+           level_send, level_recv, coarse_send, coarse_recv, square_send, square_recv, q_sem, ctx_sem):
     tokens, width = q_ref.shape
+    q_copy = pltpu.make_async_copy(q_hbm, q_ref, q_sem)
+    q_copy.start()
     heads = width // HEAD_DIM
     coarse_rows = tokens // TOP_POOL
     coarse_all = coarse_rows * n_seq
@@ -165,6 +167,12 @@
 
     tiles = tokens // QUERY_TILE
 
+    def ctx_copy(tile):
+        rows = pl.ds(pl.multiple_of(tile * QUERY_TILE, QUERY_TILE), QUERY_TILE)
+        return pltpu.make_async_copy(ctx.at[rows], ctx_hbm.at[rows], ctx_sem.at[tile])
+
+    q_copy.wait()
+
     @pl.loop(0, tiles)
     def _(tile):
         block = pl.ds(pl.multiple_of(tile * QUERY_TILE // BLOCK * BLOCK, BLOCK), BLOCK)
@@ -174,15 +182,16 @@
         @pl.loop(0, tiles)
         def _(tile):
             attend(tile, far[start:start + size, :width], far[start:start + size, width:], False, last)
+            if last:
+                ctx_copy(tile).start()
 
     @pl.loop(1, n_seq)
     def _(step):
         coarse_copy(step).wait()
 
     level_copies[3].wait()
-    attend_far(0, coarse_all + level_rows[8], False)
     level_copies[2].wait()
-    attend_far(far_at[4], level_rows[4], False)
+    attend_far(0, coarse_all + level_rows[8] + level_rows[4], False)
     level_copies[1].wait()
     attend_far(far_at[2], level_rows[2], True)
 
@@ -204,15 +213,23 @@
     square_total = squares[0]
     for step in range(1, n_head):
         square_total = square_total + squares[step]
-    inverse = lax.rsqrt(square_total / (width * n_head) + 1e-6)
+    inverse_ref[...] = lax.rsqrt(square_total / (width * n_head) + 1e-6)
+
+    @pl.loop(0, tiles)
+    def _(tile):
+        ctx_copy(tile).wait()
+
+
+def normalize(ctx_ref, inverse_ref, g_ref, o_ref):
+    tokens, width = ctx_ref.shape
     gain = g_ref[...].astype(jnp.float32)
     for piece in range(tokens // LANES):
         rows = pl.ds(piece * LANES, LANES)
-        turned = jnp.transpose(jnp.broadcast_to(inverse[piece:piece + 1], (LANES, LANES)))
+        turned = jnp.transpose(jnp.broadcast_to(inverse_ref[piece:piece + 1, :], (LANES, LANES)))
         for part in range(width // LANES):
             columns = pl.ds(part * LANES, LANES)
             o_ref[rows, columns] = (
-                ctx[rows, columns] * turned * gain[:, part * LANES:(part + 1) * LANES]
+                ctx_ref[rows, columns] * turned * gain[None, part * LANES:(part + 1) * LANES]
             ).astype(jnp.bfloat16)
 
 
@@ -224,12 +241,16 @@
     keys = BLOCK + level_total + coarse_all
     vmem = pl.BlockSpec(memory_space=pltpu.VMEM)
     dma = pltpu.SemaphoreType.DMA
-    return pl.pallas_call(
+    context, inverse = pl.pallas_call(
         functools.partial(kernel, n_seq, n_head),
-        out_shape=jax.ShapeDtypeStruct((tokens, width), jnp.bfloat16),
-        in_specs=[vmem] * 4,
-        out_specs=vmem,
+        out_shape=[
+            jax.ShapeDtypeStruct((tokens, width), jnp.float32),
+            jax.ShapeDtypeStruct((tokens // LANES, LANES), jnp.float32),
+        ],
+        in_specs=[pl.BlockSpec(memory_space=pl.ANY), vmem, vmem],
+        out_specs=[pl.BlockSpec(memory_space=pl.ANY), vmem],
         scratch_shapes=[
+            pltpu.VMEM((tokens, width), jnp.bfloat16),
             pltpu.VMEM((level_total, 2 * width), jnp.bfloat16),
             pltpu.VMEM((coarse_all + level_total, 2 * width), jnp.bfloat16),
             pltpu.VMEM((heads, tokens, 2 * LANES), jnp.float32),
@@ -242,6 +263,8 @@
             dma((n_seq,)),
             dma((n_head,)),
             dma((n_head,)),
+            dma,
+            dma((tokens // QUERY_TILE,)),
         ],
         compiler_params=pltpu.CompilerParams(
             collective_id=0, has_side_effects=True, vmem_limit_bytes=56 * 1024 * 1024
@@ -251,7 +274,14 @@
             bytes_accessed=8 * tokens * width,
             transcendentals=tokens * keys * heads,
         ),
-    )(query_rows, key_rows, value_rows, norm_gain.reshape(1, width))
+    )(query_rows, key_rows, value_rows)
+    return pl.pallas_call(
+        normalize,
+        out_shape=jax.ShapeDtypeStruct((tokens, width), jnp.bfloat16),
+        in_specs=[vmem] * 3,
+        out_specs=vmem,
+        compiler_params=pltpu.CompilerParams(vmem_limit_bytes=16 * 1024 * 1024),
+    )(context, inverse, norm_gain)
 
 
 def solution(mesh):

time: 77.5 us -> 68.7 us (0.89)
  Pallas kernels: 73.8 us -> 66.2 us
  local copies, waits for them, and re-layouts: 3.48 us -> 2.28 us
    pallas_call x1 -> x2, Pallas kernels: 73.8 us -> 66.2 us  [the longest x1 64.9 us: body(): pl.pallas_call(functools.partial(kernel, n_seq, n_head), out_shape=[jax.S...]
    reshape x1 -> x0, local copies, waits for them, and re-layouts: 1.22 us -> none  [body(): norm_gain.reshape(1, width)]
    unnamed x1 -> x6, local copies, waits for them, and re-layouts: 2.26 us -> 2.28 us
where the time goes in v1:
time: 68.7 us; the launch traced here: 68.5 us
  Pallas kernels  66.2 us (96%)
  local copies, waits for them, and re-layouts  2.28 us (3%)
    pallas_call x1, Pallas kernels, body(): pl.pallas_call(functools.partial(kernel, n_seq, n_head), out_shape=[jax.S...  64.9 us
    unnamed x6, local copies, waits for them, and re-layouts  2.28 us

profile of v1, /device:TPU:0, one launch (start us, length us, event | category | flops | bytes accessed | tf_op | source)
XLA Modules:
  0.0 68.5 jit_solution(6533421994950898507)
XLA Ops:
  0.0 0.0 copy-start.2
  0.0 64.9 %shard_map.46 = (f32[2048,256]{1,0:T(8,128)}, f32[16,128]{1,0:T(8,128)}) custom-call(bf16[2048,256]{1,0:T(8,128)(2,1)} %q_hbm.1, bf16[2048,256]{1,0:T(8,128)(2,1)} %k_ref.1, bf16[2048,256]{1,0:T(8,128)(2,1)} %v_ref.1), custom_call_target="tpu_custom_call" | custom-call | flops 6979321856 | bytes 4194304 | tf_op jit(solution)/shard_map/pallas_call | solution.py:244
  64.9 0.0 copy-done.2
  64.9 0.0 copy-start
  64.9 1.6 %copy-done = f32[2048,256]{1,0:T(8,128)S(1)} copy-done((f32[2048,256]{1,0:T(8,128)S(1)}, f32[2048,256]{1,0:T(8,128)}, u32[]{:S(2)}) %copy-start) | copy-done | bytes 2097176
  66.5 0.0 copy-start.1
  66.5 0.7 %copy-done.1 = f32[16,128]{1,0:T(8,128)S(1)} copy-done((f32[16,128]{1,0:T(8,128)S(1)}, f32[16,128]{1,0:T(8,128)}, u32[]{:S(2)}) %copy-start.1) | copy-done | bytes 8216
  67.2 1.3 %shard_map.47 = bf16[2048,256]{1,0:T(8,128)(2,1)} custom-call(f32[2048,256]{1,0:T(8,128)S(1)} %copy-done, f32[16,128]{1,0:T(8,128)S(1)} %copy-done.1, bf16[256]{0:T(256)(128)(2,1)S(1)} %copy-done.2), custom_call_target="tpu_custom_call" | custom-call | tf_op jit(solution)/shard_map/pallas_call | solution.py:278
Async XLA Ops:
  0.0 64.9 %copy-start.2 = (bf16[256]{0:T(256)(128)(2,1)S(1)}, bf16[256]{0:T(256)(128)(2,1)}, u32[]{:S(2)}) copy-start(bf16[256]{0:T(256)(128)(2,1)} %g_ref.1) | copy-start | bytes 1540
  64.9 1.6 %copy-start = (f32[2048,256]{1,0:T(8,128)S(1)}, f32[2048,256]{1,0:T(8,128)}, u32[]{:S(2)}) copy-start(f32[2048,256]{1,0:T(8,128)} %get-tuple-element.7.ctx_ref) | copy-start | bytes 6291460
  66.5 0.7 %copy-start.1 = (f32[16,128]{1,0:T(8,128)S(1)}, f32[16,128]{1,0:T(8,128)}, u32[]{:S(2)}) copy-start(f32[16,128]{1,0:T(8,128)} %get-tuple-element.8.inverse_ref) | copy-start | bytes 24580

commit v2 on v1

--- a/solution.py
+++ b/solution.py
@@ -14,6 +14,7 @@
 LEVELS = 3
 TOP_POOL = 32
 QUERY_TILE = 512
+WIDE_TILE = 1024
 CHUNK = 256
 LANES = 128
 LOG2E = math.log2(math.e)
@@ -60,14 +61,15 @@
 
     factors = [2**level for level in range(1, LEVELS + 1)]
     level_rows = {f: tokens // f for f in factors}
-    near_at, far_at, first_row = {}, {}, 0
+    level_at, first_row = {}, 0
     for f in reversed(factors):
-        near_at[f] = first_row
-        far_at[f] = coarse_all + first_row
+        level_at[f] = first_row
         first_row += level_rows[f]
+    coarse_at = first_row
+    my_coarse = pl.ds(pl.multiple_of(coarse_at + me_seq * coarse_rows, coarse_rows), coarse_rows)
     matrix = pool_matrix(factors + [TOP_POOL])
-    for side, source in enumerate((k_ref, v_ref)):
-        columns = pl.ds(side * width, width)
+
+    def pool(plane, source):
         held = []
         for chunk in range(tokens // CHUNK):
             pooled = jnp.dot(matrix, source[pl.ds(chunk * CHUNK, CHUNK), :],
@@ -75,30 +77,28 @@
             start = 0
             for f in factors:
                 size = CHUNK // f
-                near[pl.ds(near_at[f] + chunk * size, size), columns] = (
+                near[plane, pl.ds(level_at[f] + chunk * size, size), :] = (
                     pooled[start:start + size].astype(jnp.bfloat16))
                 start += size
             held.append(pooled[start:])
-        far[pl.ds(pl.multiple_of(me_seq * coarse_rows, coarse_rows), coarse_rows), columns] = (
-            jnp.concatenate(held, axis=0).astype(jnp.bfloat16))
-
-    pl.semaphore_wait(barrier, n_seq - 1 + n_head - 1)
-
-    def level_copy(level):
+        far[plane, my_coarse, :] = jnp.concatenate(held, axis=0).astype(jnp.bfloat16)
+
+    def level_copy(level, plane):
         f = 2**level
         distance = 2 ** (level - 1)
         partner = me_seq + distance * (1 - 2 * lax.rem(me_seq // distance, 2))
+        rows = pl.ds(level_at[f], level_rows[f])
         return pltpu.make_async_remote_copy(
-            src_ref=near.at[pl.ds(near_at[f], level_rows[f])],
-            dst_ref=far.at[pl.ds(far_at[f], level_rows[f])],
-            send_sem=level_send.at[level - 1],
-            recv_sem=level_recv.at[level - 1],
+            src_ref=near.at[plane, rows],
+            dst_ref=far.at[plane, rows],
+            send_sem=level_send.at[level - 1, plane],
+            recv_sem=level_recv.at[level - 1, plane],
             device_id=(partner, me_head),
             device_id_type=MESH,
         )
 
     def coarse_copy(step):
-        mine = far.at[pl.ds(pl.multiple_of(me_seq * coarse_rows, coarse_rows), coarse_rows)]
+        mine = far.at[:, my_coarse]
         return pltpu.make_async_remote_copy(
             src_ref=mine,
             dst_ref=mine,
@@ -108,23 +108,27 @@
             device_id_type=MESH,
         )
 
-    @pl.loop(1, n_seq)
-    def _(step):
-        coarse_copy(step).start()
-
-    level_copies = {level: level_copy(level) for level in range(1, LEVELS + 1)}
-    for level in (1, 3, 2):
-        level_copies[level].start()
+    pool(0, k_ref)
+    pl.semaphore_wait(barrier, n_seq - 1 + n_head - 1)
+    level_copies = {
+        (level, plane): level_copy(level, plane)
+        for level in range(1, LEVELS + 1) for plane in range(2)
+    }
+    for level in (1, 2, 3):
+        level_copies[level, 0].start()
+    pool(1, v_ref)
+    for level in (1, 2, 3):
+        level_copies[level, 1].start()
 
     lane_head = lax.broadcasted_iota(jnp.int32, (1, width), 1) // HEAD_DIM
     scaled_masks = [
         jnp.where(lane_head == h, 1.0 / math.sqrt(HEAD_DIM), 0.0).astype(jnp.bfloat16)
         for h in range(heads)
     ]
-    left = lax.broadcasted_iota(jnp.int32, (QUERY_TILE, LANES), 1) < HEAD_DIM
-
-    def attend(tile, keys, values, first, last):
-        rows = pl.ds(pl.multiple_of(tile * QUERY_TILE, QUERY_TILE), QUERY_TILE)
+    left = lax.broadcasted_iota(jnp.int32, (1, LANES), 1) < HEAD_DIM
+
+    def attend(tile, size, keys, values, first, last):
+        rows = pl.ds(pl.multiple_of(tile * size, size), size)
         query = q_ref[rows, :]
         ones = jnp.ones((keys.shape[0], LANES), jnp.bfloat16)
 
@@ -153,17 +157,17 @@
                 shares.append(summed[:, :LANES] / summed[:, LANES:])
             else:
                 acc[h, rows, :] = summed
-                high[h, rows, :] = jnp.broadcast_to(highest, (QUERY_TILE, LANES))
+                high[h, rows, :] = jnp.broadcast_to(highest, (size, LANES))
         if last:
-            total = jnp.zeros((QUERY_TILE, LANES), jnp.float32)
+            total = jnp.zeros((size, LANES), jnp.float32)
             for pair in range(heads // 2):
                 part = jnp.where(left, shares[2 * pair], shares[2 * pair + 1])
                 ctx[rows, pl.ds(pair * LANES, LANES)] = part
                 total += part * part
-            total = jnp.broadcast_to(jnp.sum(total, axis=-1, keepdims=True), (QUERY_TILE, LANES))
-            for piece in range(QUERY_TILE // LANES):
+            total = jnp.broadcast_to(jnp.sum(total, axis=-1, keepdims=True), (size, LANES))
+            for piece in range(size // LANES):
                 turned = jnp.transpose(total[piece * LANES:(piece + 1) * LANES])
-                squares[0, pl.ds(tile * (QUERY_TILE // LANES) + piece, 1), :] = turned[:1]
+                squares[0, pl.ds(tile * (size // LANES) + piece, 1), :] = turned[:1]
 
     tiles = tokens // QUERY_TILE
 
@@ -173,27 +177,37 @@
 
     q_copy.wait()
 
-    @pl.loop(0, tiles)
+    @pl.loop(0, tokens // WIDE_TILE)
     def _(tile):
-        block = pl.ds(pl.multiple_of(tile * QUERY_TILE // BLOCK * BLOCK, BLOCK), BLOCK)
-        attend(tile, k_ref[block, :], v_ref[block, :], True, False)
-
-    def attend_far(start, size, last):
-        @pl.loop(0, tiles)
-        def _(tile):
-            attend(tile, far[start:start + size, :width], far[start:start + size, width:], False, last)
-            if last:
-                ctx_copy(tile).start()
+        block = pl.ds(pl.multiple_of(tile * WIDE_TILE // BLOCK * BLOCK, BLOCK), BLOCK)
+        attend(tile, WIDE_TILE, k_ref[block, :], v_ref[block, :], True, False)
+
+    @pl.loop(1, n_seq)
+    def _(step):
+        coarse_copy(step).start()
+
+    for level in (3, 2):
+        for plane in range(2):
+            level_copies[level, plane].wait()
+    middle = pl.ds(0, level_at[2])
+
+    @pl.loop(0, tokens // WIDE_TILE)
+    def _(tile):
+        attend(tile, WIDE_TILE, far[0, middle, :], far[1, middle, :], False, False)
+
+    for plane in range(2):
+        level_copies[1, plane].wait()
 
     @pl.loop(1, n_seq)
     def _(step):
         coarse_copy(step).wait()
 
-    level_copies[3].wait()
-    level_copies[2].wait()
-    attend_far(0, coarse_all + level_rows[8] + level_rows[4], False)
-    level_copies[1].wait()
-    attend_far(far_at[2], level_rows[2], True)
+    rest = pl.ds(level_at[2], level_rows[2] + coarse_all)
+
+    @pl.loop(0, tiles)
+    def _(tile):
+        attend(tile, QUERY_TILE, far[0, rest, :], far[1, rest, :], False, True)
+        ctx_copy(tile).start()
 
     square_copies = [
         pltpu.make_async_remote_copy(
@@ -221,11 +235,13 @@
 
 
 def normalize(ctx_ref, inverse_ref, g_ref, o_ref):
-    tokens, width = ctx_ref.shape
+    size, width = ctx_ref.shape
     gain = g_ref[...].astype(jnp.float32)
-    for piece in range(tokens // LANES):
+    first = pl.program_id(0) * (size // LANES)
+    for piece in range(size // LANES):
         rows = pl.ds(piece * LANES, LANES)
-        turned = jnp.transpose(jnp.broadcast_to(inverse_ref[piece:piece + 1, :], (LANES, LANES)))
+        inverse = inverse_ref[pl.ds(first + piece, 1), :]
+        turned = jnp.transpose(jnp.broadcast_to(inverse, (LANES, LANES)))
         for part in range(width // LANES):
             columns = pl.ds(part * LANES, LANES)
             o_ref[rows, columns] = (
@@ -251,14 +267,14 @@
         out_specs=[pl.BlockSpec(memory_space=pl.ANY), vmem],
         scratch_shapes=[
             pltpu.VMEM((tokens, width), jnp.bfloat16),
-            pltpu.VMEM((level_total, 2 * width), jnp.bfloat16),
-            pltpu.VMEM((coarse_all + level_total, 2 * width), jnp.bfloat16),
+            pltpu.VMEM((2, level_total, width), jnp.bfloat16),
+            pltpu.VMEM((2, level_total + coarse_all, width), jnp.bfloat16),
             pltpu.VMEM((heads, tokens, 2 * LANES), jnp.float32),
             pltpu.VMEM((heads, tokens, LANES), jnp.float32),
             pltpu.VMEM((tokens, width), jnp.float32),
             pltpu.VMEM((n_head, tokens // LANES, LANES), jnp.float32),
-            dma((LEVELS,)),
-            dma((LEVELS,)),
+            dma((LEVELS, 2)),
+            dma((LEVELS, 2)),
             dma((n_seq,)),
             dma((n_seq,)),
             dma((n_head,)),
@@ -278,9 +294,10 @@
     return pl.pallas_call(
         normalize,
         out_shape=jax.ShapeDtypeStruct((tokens, width), jnp.bfloat16),
-        in_specs=[vmem] * 3,
-        out_specs=vmem,
-        compiler_params=pltpu.CompilerParams(vmem_limit_bytes=16 * 1024 * 1024),
+        grid=(tokens // QUERY_TILE,),
+        in_specs=[pl.BlockSpec((QUERY_TILE, width), lambda i: (i, 0)), vmem, vmem],
+        out_specs=pl.BlockSpec((QUERY_TILE, width), lambda i: (i, 0)),
+        compiler_params=pltpu.CompilerParams(vmem_limit_bytes=60 * 1024 * 1024),
     )(context, inverse, norm_gain)
 
 

time: 68.7 us -> 70.6 us (1.028)
  Pallas kernels: 66.2 us -> 70.4 us
  local copies, waits for them, and re-layouts: 2.28 us -> 0 us
    pallas_call x1, Pallas kernels: 1.31 us -> 3.82 us  [body(): pl.pallas_call(normalize, out_shape=jax.ShapeDtypeStruct((tokens, width),...]
    unnamed x6 -> x0, local copies, waits for them, and re-layouts: 2.28 us -> none
    pallas_call x1, Pallas kernels: 64.9 us -> 66.5 us  [body(): pl.pallas_call(functools.partial(kernel, n_seq, n_head), out_shape=[jax.S...]
where the time goes in v2:
time: 70.6 us; the launch traced here: 70.4 us
  Pallas kernels  70.4 us (100%)
    pallas_call x1, Pallas kernels, body(): pl.pallas_call(functools.partial(kernel, n_seq, n_head), out_shape=[jax.S...  66.5 us
    pallas_call x1, Pallas kernels, body(): pl.pallas_call(normalize, out_shape=jax.ShapeDtypeStruct((tokens, width),...  3.82 us

profile of v2, /device:TPU:0, one launch (start us, length us, event | category | flops | bytes accessed | tf_op | source)
XLA Modules:
  0.0 70.4 jit_solution(6851965511763093279)
XLA Ops:
  0.0 66.5 %shard_map.46 = (f32[2048,256]{1,0:T(8,128)}, f32[16,128]{1,0:T(8,128)}) custom-call(bf16[2048,256]{1,0:T(8,128)(2,1)} %q_hbm.1, bf16[2048,256]{1,0:T(8,128)(2,1)} %k_ref.1, bf16[2048,256]{1,0:T(8,128)(2,1)} %v_ref.1), custom_call_target="tpu_custom_call" | custom-call | flops 6979321856 | bytes 4194304 | tf_op jit(solution)/shard_map/pallas_call | solution.py:260
  66.5 3.8 %shard_map.47 = bf16[2048,256]{1,0:T(8,128)(2,1)} custom-call(f32[2048,256]{1,0:T(8,128)} %get-tuple-element.7.ctx_ref, f32[16,128]{1,0:T(8,128)} %get-tuple-element.8.inverse_ref, bf16[256]{0:T(256)(128)(2,1)} %g_ref.1), custom_call_target="tpu_custom_call" | custom-call | tf_op jit(solution)/shard_map/pallas_call | solution.py:294

commit v3 on v2

--- a/solution.py
+++ b/solution.py
@@ -119,6 +119,10 @@
     pool(1, v_ref)
     for level in (1, 2, 3):
         level_copies[level, 1].start()
+
+    @pl.loop(1, n_seq)
+    def _(step):
+        coarse_copy(step).start()
 
     lane_head = lax.broadcasted_iota(jnp.int32, (1, width), 1) // HEAD_DIM
     scaled_masks = [
@@ -182,10 +186,6 @@
         block = pl.ds(pl.multiple_of(tile * WIDE_TILE // BLOCK * BLOCK, BLOCK), BLOCK)
         attend(tile, WIDE_TILE, k_ref[block, :], v_ref[block, :], True, False)
 
-    @pl.loop(1, n_seq)
-    def _(step):
-        coarse_copy(step).start()
-
     for level in (3, 2):
         for plane in range(2):
             level_copies[level, plane].wait()
@@ -235,13 +235,11 @@
 
 
 def normalize(ctx_ref, inverse_ref, g_ref, o_ref):
-    size, width = ctx_ref.shape
+    tokens, width = ctx_ref.shape
     gain = g_ref[...].astype(jnp.float32)
-    first = pl.program_id(0) * (size // LANES)
-    for piece in range(size // LANES):
+    for piece in range(tokens // LANES):
         rows = pl.ds(piece * LANES, LANES)
-        inverse = inverse_ref[pl.ds(first + piece, 1), :]
-        turned = jnp.transpose(jnp.broadcast_to(inverse, (LANES, LANES)))
+        turned = jnp.transpose(jnp.broadcast_to(inverse_ref[piece:piece + 1, :], (LANES, LANES)))
         for part in range(width // LANES):
             columns = pl.ds(part * LANES, LANES)
             o_ref[rows, columns] = (
@@ -294,10 +292,9 @@
     return pl.pallas_call(
         normalize,
         out_shape=jax.ShapeDtypeStruct((tokens, width), jnp.bfloat16),
-        grid=(tokens // QUERY_TILE,),
-        in_specs=[pl.BlockSpec((QUERY_TILE, width), lambda i: (i, 0)), vmem, vmem],
-        out_specs=pl.BlockSpec((QUERY_TILE, width), lambda i: (i, 0)),
-        compiler_params=pltpu.CompilerParams(vmem_limit_bytes=60 * 1024 * 1024),
+        in_specs=[vmem] * 3,
+        out_specs=vmem,
+        compiler_params=pltpu.CompilerParams(vmem_limit_bytes=16 * 1024 * 1024),
     )(context, inverse, norm_gain)
 
 

time: 70.6 us -> 70.6 us (level)
  Pallas kernels: 70.4 us -> 68.1 us
  local copies, waits for them, and re-layouts: 0 us -> 2.28 us
    pallas_call x1, Pallas kernels: 3.82 us -> 1.31 us  [body(): pl.pallas_call(normalize, out_shape=jax.ShapeDtypeStruct((tokens, width),...]
    unnamed x0 -> x6, local copies, waits for them, and re-layouts: none -> 2.28 us
where the time goes in v3:
time: 70.6 us; the launch traced here: 70.4 us
  Pallas kernels  68.1 us (96%)
  local copies, waits for them, and re-layouts  2.28 us (3%)
    pallas_call x1, Pallas kernels, body(): pl.pallas_call(functools.partial(kernel, n_seq, n_head), out_shape=[jax.S...  66.8 us
    unnamed x6, local copies, waits for them, and re-layouts  2.28 us

profile of v3, /device:TPU:0, one launch (start us, length us, event | category | flops | bytes accessed | tf_op | source)
XLA Modules:
  0.0 70.4 jit_solution(16634636703839803504)
XLA Ops:
  0.0 0.0 copy-start.2
  0.0 66.8 %shard_map.46 = (f32[2048,256]{1,0:T(8,128)}, f32[16,128]{1,0:T(8,128)}) custom-call(bf16[2048,256]{1,0:T(8,128)(2,1)} %q_hbm.1, bf16[2048,256]{1,0:T(8,128)(2,1)} %k_ref.1, bf16[2048,256]{1,0:T(8,128)(2,1)} %v_ref.1), custom_call_target="tpu_custom_call" | custom-call | flops 6979321856 | bytes 4194304 | tf_op jit(solution)/shard_map/pallas_call | solution.py:258
  66.8 0.0 copy-done.2
  66.8 0.0 copy-start
  66.8 1.6 %copy-done = f32[2048,256]{1,0:T(8,128)S(1)} copy-done((f32[2048,256]{1,0:T(8,128)S(1)}, f32[2048,256]{1,0:T(8,128)}, u32[]{:S(2)}) %copy-start) | copy-done | bytes 2097176
  68.4 0.0 copy-start.1
  68.4 0.7 copy-done.1
  69.1 1.3 %shard_map.47 = bf16[2048,256]{1,0:T(8,128)(2,1)} custom-call(f32[2048,256]{1,0:T(8,128)S(1)} %copy-done, f32[16,128]{1,0:T(8,128)S(1)} %copy-done.1, bf16[256]{0:T(256)(128)(2,1)S(1)} %copy-done.2), custom_call_target="tpu_custom_call" | custom-call | tf_op jit(solution)/shard_map/pallas_call | solution.py:292
Async XLA Ops:
  0.0 66.8 %copy-start.2 = (bf16[256]{0:T(256)(128)(2,1)S(1)}, bf16[256]{0:T(256)(128)(2,1)}, u32[]{:S(2)}) copy-start(bf16[256]{0:T(256)(128)(2,1)} %g_ref.1) | copy-start | bytes 1540
  66.8 1.6 %copy-start = (f32[2048,256]{1,0:T(8,128)S(1)}, f32[2048,256]{1,0:T(8,128)}, u32[]{:S(2)}) copy-start(f32[2048,256]{1,0:T(8,128)} %get-tuple-element.7.ctx_ref) | copy-start | bytes 6291460
  68.4 0.7 copy-start.1

commit v4 on v1

--- a/solution.py
+++ b/solution.py
@@ -84,15 +84,17 @@
 
     pl.semaphore_wait(barrier, n_seq - 1 + n_head - 1)
 
-    def level_copy(level):
+    def level_copy(level, half=0):
         f = 2**level
+        size = level_rows[f] // 2 if level == 1 else level_rows[f]
+        slot = half * LEVELS + level - 1 if level == 1 else level - 1
         distance = 2 ** (level - 1)
         partner = me_seq + distance * (1 - 2 * lax.rem(me_seq // distance, 2))
         return pltpu.make_async_remote_copy(
-            src_ref=near.at[pl.ds(near_at[f], level_rows[f])],
-            dst_ref=far.at[pl.ds(far_at[f], level_rows[f])],
-            send_sem=level_send.at[level - 1],
-            recv_sem=level_recv.at[level - 1],
+            src_ref=near.at[pl.ds(near_at[f] + half * size, size)],
+            dst_ref=far.at[pl.ds(far_at[f] + half * size, size)],
+            send_sem=level_send.at[slot],
+            recv_sem=level_recv.at[slot],
             device_id=(partner, me_head),
             device_id_type=MESH,
         )
@@ -108,13 +110,17 @@
             device_id_type=MESH,
         )
 
+    level_copies = {level: level_copy(level) for level in range(1, LEVELS + 1)}
+    later_half = level_copy(1, 1)
+    level_copies[1].start()
+
     @pl.loop(1, n_seq)
     def _(step):
         coarse_copy(step).start()
 
-    level_copies = {level: level_copy(level) for level in range(1, LEVELS + 1)}
-    for level in (1, 3, 2):
+    for level in (3, 2):
         level_copies[level].start()
+    later_half.start()
 
     lane_head = lax.broadcasted_iota(jnp.int32, (1, width), 1) // HEAD_DIM
     scaled_masks = [
@@ -193,7 +199,9 @@
     level_copies[2].wait()
     attend_far(0, coarse_all + level_rows[8] + level_rows[4], False)
     level_copies[1].wait()
-    attend_far(far_at[2], level_rows[2], True)
+    attend_far(far_at[2], level_rows[2] // 2, False)
+    later_half.wait()
+    attend_far(far_at[2] + level_rows[2] // 2, level_rows[2] // 2, True)
 
     square_copies = [
         pltpu.make_async_remote_copy(
@@ -257,8 +265,8 @@
             pltpu.VMEM((heads, tokens, LANES), jnp.float32),
             pltpu.VMEM((tokens, width), jnp.float32),
             pltpu.VMEM((n_head, tokens // LANES, LANES), jnp.float32),
-            dma((LEVELS,)),
-            dma((LEVELS,)),
+            dma((LEVELS + 1,)),
+            dma((LEVELS + 1,)),
             dma((n_seq,)),
             dma((n_seq,)),
             dma((n_head,)),

time: 68.7 us -> 81.4 us (1.18)
  Pallas kernels: 66.2 us -> 78.9 us
    pallas_call x1, Pallas kernels: 64.9 us -> 77.6 us  [body(): pl.pallas_call(functools.partial(kernel, n_seq, n_head), out_shape=[jax.S...]
where the time goes in v4:
time: 81.4 us; the launch traced here: 81.2 us
  Pallas kernels  78.9 us (97%)
  local copies, waits for them, and re-layouts  2.28 us (3%)
    pallas_call x1, Pallas kernels, body(): pl.pallas_call(functools.partial(kernel, n_seq, n_head), out_shape=[jax.S...  77.6 us
    unnamed x6, local copies, waits for them, and re-layouts  2.28 us

profile of v4, /device:TPU:0, one launch (start us, length us, event | category | flops | bytes accessed | tf_op | source)
XLA Modules:
  0.0 81.2 jit_solution(1632967179407214979)
XLA Ops:
  0.0 0.0 copy-start.2
  0.0 77.6 %shard_map.46 = (f32[2048,256]{1,0:T(8,128)}, f32[16,128]{1,0:T(8,128)}) custom-call(bf16[2048,256]{1,0:T(8,128)(2,1)} %q_hbm.1, bf16[2048,256]{1,0:T(8,128)(2,1)} %k_ref.1, bf16[2048,256]{1,0:T(8,128)(2,1)} %v_ref.1), custom_call_target="tpu_custom_call" | custom-call | flops 6979321856 | bytes 4194304 | tf_op jit(solution)/shard_map/pallas_call | solution.py:252
  77.6 0.0 copy-done.2
  77.6 0.0 copy-start
  77.6 1.6 %copy-done = f32[2048,256]{1,0:T(8,128)S(1)} copy-done((f32[2048,256]{1,0:T(8,128)S(1)}, f32[2048,256]{1,0:T(8,128)}, u32[]{:S(2)}) %copy-start) | copy-done | bytes 2097176
  79.2 0.0 copy-start.1
  79.2 0.7 copy-done.1
  79.9 1.3 %shard_map.47 = bf16[2048,256]{1,0:T(8,128)(2,1)} custom-call(f32[2048,256]{1,0:T(8,128)S(1)} %copy-done, f32[16,128]{1,0:T(8,128)S(1)} %copy-done.1, bf16[256]{0:T(256)(128)(2,1)S(1)} %copy-done.2), custom_call_target="tpu_custom_call" | custom-call | tf_op jit(solution)/shard_map/pallas_call | solution.py:286
Async XLA Ops:
  0.0 77.6 %copy-start.2 = (bf16[256]{0:T(256)(128)(2,1)S(1)}, bf16[256]{0:T(256)(128)(2,1)}, u32[]{:S(2)}) copy-start(bf16[256]{0:T(256)(128)(2,1)} %g_ref.1) | copy-start | bytes 1540
  77.6 1.6 %copy-start = (f32[2048,256]{1,0:T(8,128)S(1)}, f32[2048,256]{1,0:T(8,128)}, u32[]{:S(2)}) copy-start(f32[2048,256]{1,0:T(8,128)} %get-tuple-element.7.ctx_ref) | copy-start | bytes 6291460
  79.2 0.7 copy-start.1
